TPU v7x, 32 devices: a whole 2x2x4 slice. The times are simulated.
32 devices in a mesh: pair: 8 (over z, core), aux: 4 (over y, x).
Axes of the slice: x: 2, y: 2, z: 4, core: 2. Of those that a mesh axis runs over, the one named last changes fastest.
Arguments:
- c_occ: bfloat16 [12288, 1024], P('pair', 'aux'), may hold values from -0.1875 to 0.1875
- c_vir: bfloat16 [12288, 11264], P('pair', 'aux'), may hold values from -0.0546875 to 0.0546875
- e_occ: float32 [1024], P('aux'), may hold values from -2 to -0.3
- e_vir: float32 [11264], P('aux'), may hold values from 0.2 to 3
- tau_points: float32 [2], replicated, may hold values from 0.2 to 2
- pair_blocks: int32 [32, 2], P('pair'), may hold values from 0 to 767
- block_count: int32 [8], P('pair'), may hold values from 1 to 4, 20 in all
- three_center: bfloat16 [9216, 32, 256], P('aux', 'pair'), may hold values from -0.59765625 to 0.59765625
Outputs:
- coupling: float32 [9216, 2, 512], P(('aux', 'pair'))
Inputs may be any that keep to these rules, and one draw needn't show every extreme that they name: pair_blocks[s] names the AO shell blocks of the rows and the columns of slot s. Slots s with s mod 4 < block_count[s // 4] are live, the others are ignored; some index of pair has all 4 slots live.
All inputs are finite; a program needn't handle non-finite values. No bound on the sum of `block_count` on one device may be relied on, other than what follows from the above.
Results may differ from a plain program's by a relative error of at most 0.0046.
Values may be sent and summed in bfloat16 or wider, within the bound.
A program may use at most 128 MiB of HBM per device.

v0:
```python
import functools

import jax
import jax.numpy as jnp
from jax import lax
from jax.experimental import pallas as pl
from jax.experimental.pallas import tpu as pltpu
from jax.sharding import PartitionSpec as P

BS = 16
TAUS = 2
WIN_DEV = 128
PAIRS = 2
HOP = 2
MESH = pl.DeviceIdType.MESH
VMEM = pl.BlockSpec(memory_space=pltpu.VMEM)
DMA = pltpu.SemaphoreType.DMA
BF16 = jnp.bfloat16
F32 = jnp.float32


def params(collective_id):
    return pltpu.CompilerParams(
        collective_id=collective_id, has_side_effects=True, vmem_limit_bytes=40 * 2**20
    )


def greet(pair_peers, aux_peers=()):
    barrier = pltpu.get_barrier_semaphore()
    for peer in pair_peers:
        pl.semaphore_signal(barrier, inc=1, device_id={"pair": peer}, device_id_type=MESH)
    for peer in aux_peers:
        pl.semaphore_signal(barrier, inc=1, device_id={"aux": peer}, device_id_type=MESH)
    pl.semaphore_wait(barrier, len(pair_peers) + len(aux_peers))


def remote(source, target, send, received, axis, device):
    return pltpu.make_async_remote_copy(
        src_ref=source,
        dst_ref=target,
        send_sem=send,
        recv_sem=received,
        device_id={axis: device},
        device_id_type=MESH,
    )


def place():
    me = lax.axis_index("pair")
    core = lax.rem(me, 2)
    return me, core, me // 2, me + 1 - 2 * core


def table_kernel(groups, mine, out, send, received):
    me = lax.axis_index("pair")
    peers = [lax.rem(me + k, groups) for k in range(1, groups)]
    greet(peers)
    copies = []
    for k in range(groups - 1):
        copy = remote(mine, out.at[me], send.at[k], received.at[k], "pair", peers[k])
        copy.start()
        copies.append(copy)
    out[me] = mine[...]
    for copy in copies:
        copy.wait()


def gather_table(table, groups):
    return pl.pallas_call(
        functools.partial(table_kernel, groups),
        out_shape=jax.ShapeDtypeStruct((groups,) + table.shape, table.dtype),
        in_specs=[VMEM],
        out_specs=VMEM,
        scratch_shapes=[DMA((groups - 1,)), DMA((groups - 1,))],
        compiler_params=params(0),
    )(table)


def rows_kernel(chips, chunks, rows, window, out, blocks,
                own, right_in, left_in, right_out, left_out,
                own_send, own_recv, right_send, right_recv, left_send, left_recv,
                done_send, done_recv, far_send, far_recv, near_send, near_recv):
    me, core, chip, partner = place()
    last = chips - 1
    after = lax.rem(me + 2, 2 * chips)
    before = lax.rem(me + 2 * chips - 2, 2 * chips)
    line = [lax.rem(chip + k, chips) * 2 + core for k in range(1, chips)]
    greet([partner] + line)

    def swap(j):
        return remote(rows.at[1 - core, j], own.at[j], own_send.at[j], own_recv.at[j], "pair", partner)

    def rightward(j):
        return remote(right_out.at[j], right_in.at[j], right_send.at[j], right_recv.at[j], "pair", after)

    def leftward(j):
        return remote(left_out.at[j], left_in.at[j], left_send.at[j], left_recv.at[j], "pair", before)

    def finished(j):
        return remote(out.at[core, j], out.at[core, j], done_send.at[j], done_recv.at[j], "pair", partner)

    def start_swap(j, carry):
        swap(j).start()
        return carry

    lax.fori_loop(0, chunks, start_swap, 0)
    far = []
    for k, peer in enumerate(line):
        far.append(remote(window, blocks.at[me], far_send.at[k], far_recv.at[k], "pair", peer))
    near = [remote(window, blocks.at[me], near_send.at[0], near_recv.at[0], "pair", partner)]
    near[0].start()
    blocks[me] = window[...]

    def step(i, carry):
        @pl.when(i < chunks)
        def _():
            swap(i).wait_recv()
            own[i] = own[i] + rows[core, i]

        to_right = i - HOP * chip

        @pl.when((to_right >= 0) & (to_right < chunks))
        def _():
            @pl.when(chip > 0)
            def _():
                rightward(to_right).wait_recv()

            @pl.when(chip == 0)
            def _():
                right_out[to_right] = own[to_right]

            @pl.when((chip > 0) & (chip < last))
            def _():
                right_out[to_right] = own[to_right] + right_in[to_right]

            @pl.when(chip < last)
            def _():
                rightward(to_right).start()

        to_left = i - HOP * (last - chip)

        @pl.when((to_left >= 0) & (to_left < chunks))
        def _():
            @pl.when(chip < last)
            def _():
                leftward(to_left).wait_recv()

            @pl.when(chip == last)
            def _():
                left_out[to_left] = own[to_left]

            @pl.when((chip > 0) & (chip < last))
            def _():
                left_out[to_left] = own[to_left] + left_in[to_left]

            @pl.when(chip > 0)
            def _():
                leftward(to_left).start()

        ready = i - HOP * jnp.maximum(chip, last - chip)

        @pl.when((ready >= 0) & (ready < chunks))
        def _():
            @pl.when(chip == 0)
            def _():
                out[core, ready] = own[ready] + left_in[ready]

            @pl.when(chip == last)
            def _():
                out[core, ready] = own[ready] + right_in[ready]

            @pl.when((chip > 0) & (chip < last))
            def _():
                out[core, ready] = own[ready] + left_in[ready] + right_in[ready]

            finished(ready).start()

        return carry

    lax.fori_loop(0, HOP * last, step, 0)
    for copy in far:
        copy.start()
    lax.fori_loop(HOP * last, chunks + HOP * last, step, 0)
    for k, copy in enumerate(far):
        copy.wait_recv()
        origin = lax.rem(chip + last - k, chips) * 2 + core
        pass_on = remote(
            blocks.at[origin], blocks.at[origin], near_send.at[k + 1], near_recv.at[k + 1], "pair", partner
        )
        pass_on.start()
        near.append(pass_on)

    def drain(j, carry):
        swap(j).wait_send()

        @pl.when(chip < last)
        def _():
            rightward(j).wait_send()

        @pl.when(chip > 0)
        def _():
            leftward(j).wait_send()

        finished(j).wait_send()
        remote(
            out.at[1 - core, j], out.at[1 - core, j], done_send.at[j], done_recv.at[j], "pair", partner
        ).wait_recv()
        return carry

    lax.fori_loop(0, chunks, drain, 0)
    for copy in near:
        copy.wait()
    for copy in far:
        copy.wait_send()


def sum_rows(rows, window, groups):
    chunks = rows.shape[0] // (2 * BS)
    width = rows.shape[1]
    shape = (2, chunks, BS, width)
    chips = groups // 2
    summed, blocks = pl.pallas_call(
        functools.partial(rows_kernel, chips, chunks),
        out_shape=(
            jax.ShapeDtypeStruct(shape, rows.dtype),
            jax.ShapeDtypeStruct((groups,) + window.shape, window.dtype),
        ),
        in_specs=[VMEM, VMEM],
        out_specs=(VMEM, VMEM),
        scratch_shapes=[pltpu.VMEM(shape[1:], rows.dtype)] * 5
        + [DMA((chunks,))] * 8
        + [DMA((chips - 1,))] * 2
        + [DMA((chips,))] * 2,
        compiler_params=params(1),
    )(rows.reshape(shape), window)
    return summed.reshape(rows.shape), blocks


def tiles_kernel(shards, terms, tiles, held, term_send, term_recv, tile_send, tile_recv):
    shard = lax.axis_index("aux")
    peers = [flipped(shard, k, shards) for k in range(1, shards)]
    greet([], peers)
    parts = []
    for k, peer in enumerate(peers):
        copy = remote(terms.at[peer], held.at[k], term_send.at[k], term_recv.at[k], "aux", peer)
        copy.start()
        parts.append(copy)
    total = terms[shard]
    for k, copy in enumerate(parts):
        copy.wait_recv()
        total = total + held[k]
    tiles[shard] = total.astype(tiles.dtype)
    sums = []
    for k, peer in enumerate(peers):
        copy = remote(tiles.at[shard], tiles.at[shard], tile_send.at[k], tile_recv.at[k], "aux", peer)
        copy.start()
        sums.append(copy)
    for copy in sums:
        copy.wait()
    for copy in parts:
        copy.wait_send()


def sum_tiles(terms, shards):
    rows, width = terms.shape
    grouped = (shards, rows // shards, width)
    tiles = pl.pallas_call(
        functools.partial(tiles_kernel, shards),
        out_shape=jax.ShapeDtypeStruct(grouped, BF16),
        in_specs=[VMEM],
        out_specs=VMEM,
        scratch_shapes=[pltpu.VMEM((shards - 1,) + grouped[1:], F32)] + [DMA((shards - 1,))] * 4,
        compiler_params=params(2),
    )(terms.reshape(grouped))
    return tiles.reshape(rows, width)


def flipped(shard, k, shards):
    other, bit = 0, 1
    while bit < shards:
        other = other + lax.rem(shard // bit + k // bit, 2) * bit
        bit = bit * 2
    return other


def coupling_kernel(chips, shards, blocks, mine, out, kept, moved, near_out, near_in, leaving, arriving,
                    moved_send, moved_recv, near_send, near_recv, far_send, far_recv):
    me, core, chip, partner = place()
    shard = lax.axis_index("aux")
    last = chips - 1
    peers = [flipped(shard, k, shards) for k in range(1, shards)]
    greet([partner] + [lax.rem(chip + k, chips) * 2 + core for k in range(1, chips)], peers)

    def arrival(k):
        return remote(
            mine, moved.at[k], moved_send.at[k], moved_recv.at[k], "aux", flipped(shard, k, shards)
        )

    def target(j):
        return lax.rem(chip + 1 + j, chips)

    def swap(k, j):
        return remote(
            near_out.at[k, j], near_in.at[k, j], near_send.at[k, j], near_recv.at[k, j], "pair", partner
        )

    def hand_over(k, j):
        return remote(
            leaving.at[k, j], arriving.at[k, j], far_send.at[k, j], far_recv.at[k, j],
            "pair", target(j) * 2 + core,
        )

    for k in range(1, shards):
        arrival(k).start()
    moved[0] = mine[...]

    def product(j, to_core, right):
        left = blocks[target(j), to_core]
        return lax.dot_general(left, right, (((1,), (1,)), ((), ())), preferred_element_type=F32)

    def chunk(k, carry):
        @pl.when(k > 0)
        def _():
            arrival(k).wait_recv()

        def for_partner(j, carry):
            near_out[k, j] = product(j, 1 - core, moved[k]).astype(near_out.dtype)
            swap(k, j).start()
            return carry

        lax.fori_loop(0, chips, for_partner, 0)

        def for_line(j, carry):
            term = product(j, core, moved[k])
            swap(k, j).wait_recv()
            leaving[k, j] = (term + near_in[k, j].astype(F32)).astype(leaving.dtype)
            hand_over(k, j).start()
            return carry

        lax.fori_loop(0, last, for_line, 0)
        term = product(last, core, moved[k])
        swap(k, last).wait_recv()
        kept[k] = term + near_in[k, last].astype(F32)
        return carry

    lax.fori_loop(0, shards, chunk, 0)

    def collect(k, carry):
        total = kept[k]
        for j in range(last):
            hand_over(k, j).wait_recv()
            total = total + arriving[k, j].astype(F32)
        width = total.shape[1] // TAUS
        for t in range(TAUS):
            column = (t * shards + flipped(shard, k, shards)) * width
            out[:, pl.ds(pl.multiple_of(column, width), width)] = total[:, t * width:(t + 1) * width]
        for j in range(last):
            hand_over(k, j).wait_send()
        for j in range(chips):
            swap(k, j).wait_send()

        @pl.when(k > 0)
        def _():
            arrival(k).wait_send()

        return carry

    lax.fori_loop(0, shards, collect, 0)


def couple(blocks, moved, groups, shards):
    chips = groups // 2
    rows, depth = blocks.shape
    block = (rows // groups, moved.shape[0])
    return pl.pallas_call(
        functools.partial(coupling_kernel, chips, shards),
        out_shape=jax.ShapeDtypeStruct((block[0], shards * block[1]), F32),
        in_specs=[VMEM, VMEM],
        out_specs=VMEM,
        scratch_shapes=[
            pltpu.VMEM((shards,) + block, F32),
            pltpu.VMEM((shards,) + moved.shape, BF16),
            pltpu.VMEM((shards, chips) + block, BF16),
            pltpu.VMEM((shards, chips) + block, BF16),
            pltpu.VMEM((shards, chips - 1) + block, BF16),
            pltpu.VMEM((shards, chips - 1) + block, BF16),
        ]
        + [DMA((shards,))] * 2
        + [DMA((shards, chips))] * 2
        + [DMA((shards, chips - 1))] * 2,
        compiler_params=params(3),
    )(blocks.reshape(chips, 2, block[0], depth), moved)


def moved_kernel(own_slots, slots_ref, occ, vir, blocks, out, half):
    live_total, size, width = occ.shape
    fold_rows = blocks.shape[2]
    pairs = fold_rows // (own_slots * size)
    wide = pairs * width
    rank = lax.broadcasted_iota(jnp.int32, (pairs * own_slots, size, wide), 0)
    side = lax.broadcasted_iota(jnp.int32, (pairs * own_slots, size, wide), 2) // width

    def one_slot(n, carry):
        slot = slots_ref[n]
        tile = occ[n].astype(F32)
        spread = jnp.concatenate([tile] * pairs, axis=1)[None]
        spread = jnp.where(rank == side * own_slots + lax.rem(slot, own_slots), spread, 0.0)
        spread = spread.reshape(fold_rows, wide).astype(BF16)
        half[n] = jnp.dot(
            blocks[slot // own_slots], spread, preferred_element_type=F32
        ).astype(BF16)
        return carry

    lax.fori_loop(0, live_total, one_slot, 0)
    row = lax.broadcasted_iota(jnp.int32, (width, wide), 0) // size
    column = lax.rem(lax.broadcasted_iota(jnp.int32, (width, wide), 1), width) // size
    same = row == column
    entry = lax.broadcasted_iota(jnp.int32, (pairs * size, wide), 0)
    lane = lax.broadcasted_iota(jnp.int32, (pairs * size, wide), 1)
    fold = jnp.where(entry == lane // width * size + lax.rem(lane, size), 1.0, 0.0).astype(BF16)

    def one_pair(at, carry):
        rows = pl.ds(pl.multiple_of(at * size, size), size)
        right = half[:, rows, :].reshape(live_total * size, wide)
        summed = jnp.dot(vir[...], right, preferred_element_type=F32)
        summed = jnp.where(same, summed, 0.0).astype(BF16)
        out[at] = lax.dot_general(
            fold, summed, (((1,), (1,)), ((), ())), preferred_element_type=F32
        ).astype(BF16)
        return carry

    lax.fori_loop(0, out.shape[0], one_pair, 0, unroll=4)


def move(slots, occ, vir, blocks, own_slots):
    live_total, size, width = occ.shape
    wide = blocks.shape[2] // (own_slots * size) * width
    rows = blocks.shape[1]
    return pl.pallas_call(
        functools.partial(moved_kernel, own_slots),
        out_shape=jax.ShapeDtypeStruct((rows // size, wide // width * size, width), BF16),
        in_specs=[pl.BlockSpec(memory_space=pltpu.SMEM), VMEM, VMEM, VMEM],
        out_specs=VMEM,
        scratch_shapes=[pltpu.VMEM((live_total, rows, wide), BF16)],
        compiler_params=pltpu.CompilerParams(vmem_limit_bytes=40 * 2**20),
    )(slots, occ, vir, blocks)


def owned_rows(coefficient, names, group):
    local_blocks = coefficient.shape[0] // BS
    blocks = coefficient.reshape(local_blocks, BS, coefficient.shape[1])
    local_names = names - group * local_blocks
    owned = (local_names >= 0) & (local_names < local_blocks)
    picked = jnp.take(blocks, jnp.clip(local_names, 0, local_blocks - 1), axis=0)
    picked = jnp.where(owned[:, None, None], picked, jnp.zeros((), BF16))
    return picked.reshape(names.shape[0] * BS, coefficient.shape[1])


def own_gram(rows, energy, exponent_sign, tau_points, picks):
    factor = jnp.exp(exponent_sign * tau_points[:, None] * energy[None, :] / 2.0)
    scaled = (rows[None].astype(F32) * factor[:, None, :]).astype(BF16)
    own = jnp.concatenate(
        [lax.dynamic_slice_in_dim(scaled, pick * BS, BS, 1) for pick in picks], axis=1
    )
    return jnp.einsum("tin,tjn->tij", own, scaled, preferred_element_type=F32)


def per_device(groups, shards, c_occ, c_vir, e_occ, e_vir, tau_points, pair_blocks, block_count,
               three_center):
    own_slots = pair_blocks.shape[0]
    slot_total = own_slots * groups
    live_total = 5 * groups // 2
    group = lax.axis_index("pair")
    fields = 2 * own_slots + 1
    flat = jnp.concatenate([pair_blocks.reshape(-1), block_count])
    table = jnp.zeros((8, 128), jnp.int32).at[0, :fields].set(flat)
    tables = gather_table(table, groups)[:, 0, :fields]
    names = tables[:, :-1].reshape(slot_total, 2)
    counts = tables[:, -1]
    live = (jnp.arange(own_slots)[None, :] < counts[:, None]).reshape(slot_total)
    ids = jnp.arange(slot_total)
    ranks = jnp.sum(jnp.where(live[None, :] & (ids[None, :] < ids[:, None]), 1, 0), axis=1)
    select = live[None, :] & (ranks[None, :] == jnp.arange(live_total)[:, None])
    live_names = jnp.sum(jnp.where(select[:, :, None], names[None], 0), axis=1)
    rows = jnp.concatenate(
        [owned_rows(c_occ, live_names[:, 0], group), owned_rows(c_vir, live_names[:, 1], group)], axis=1
    )
    flat_blocks = three_center.reshape(three_center.shape[0], own_slots * BS * BS)
    window = three_center[:WIN_DEV].reshape(PAIRS, WIN_DEV // PAIRS, own_slots, BS, BS)
    window = window.transpose(1, 4, 0, 2, 3).reshape(WIN_DEV // PAIRS * BS, PAIRS * own_slots * BS)
    rows, blocks = sum_rows(rows, window, groups)
    before = jnp.sum(jnp.where(jnp.arange(groups) < group, counts, 0))
    picks = [jnp.minimum(before + k, live_total - 1) for k in range(own_slots)]
    n_occ = c_occ.shape[1]
    terms = jnp.concatenate(
        [
            own_gram(rows[:, :n_occ], e_occ, 1.0, tau_points, picks),
            own_gram(rows[:, n_occ:], e_vir, -1.0, tau_points, picks),
        ],
        axis=0,
    )
    tiles = sum_tiles(terms.reshape(2 * TAUS * own_slots * BS, live_total * BS), shards)
    width = TAUS * own_slots * BS
    live_ids = jnp.sum(jnp.where(select, ids[None, :], 0), axis=1)
    occ_tiles = tiles[:width].T.reshape(live_total, BS, width)
    moved = move(live_ids, occ_tiles, tiles[width:], blocks, own_slots)
    moved = moved.reshape(WIN_DEV // PAIRS, PAIRS, BS, TAUS, own_slots, BS)
    live_mask = jnp.arange(own_slots) < block_count[0]
    moved = jnp.where(live_mask[:, None], moved, jnp.zeros((), BF16))
    transformed = moved.transpose(3, 1, 0, 4, 2, 5).reshape(TAUS * WIN_DEV, own_slots * BS * BS)
    coupling = couple(flat_blocks, transformed, groups, shards)
    return coupling.reshape(coupling.shape[0], TAUS, shards * WIN_DEV)


def solution(mesh):
    placed = (
        P("pair", "aux"),
        P("pair", "aux"),
        P("aux"),
        P("aux"),
        P(),
        P("pair", None),
        P("pair"),
        P("aux", "pair", None),
    )
    return jax.shard_map(
        functools.partial(per_device, mesh.shape["pair"], mesh.shape["aux"]),
        mesh=mesh,
        in_specs=placed,
        out_specs=P(("aux", "pair"), None, None),
        check_vma=False,
    )
```

profile of v0, /device:TPU:0, one launch (start us, length us, event | category | flops | bytes accessed | tf_op | source)
XLA Modules:
  0.0 204.4 jit_solution(3905250017330427264)
XLA Ops:
  0.7 0.4 copy-done
  1.2 0.7 broadcast_multiply_fusion
  1.8 0.8 multiply_exponential_fusion.1
  2.6 0.8 copy.30
  3.5 0.8 multiply_exponential_fusion
  4.3 7.4 %shard_map.82 = s32[8,8,128]{2,1,0:T(8,128)S(1)} custom-call(s32[8,128]{1,0:T(8,128)S(1)} %scatter.4.mine), custom_call_target="tpu_custom_call" | custom-call | tf_op jit(solution)/shard_map/pallas_call | solution.py:69
  12.0 0.6 fusion.20
  15.8 0.4 select_reduce_fusion
  17.0 0.6 gather_fusion
  17.5 0.8 select_select_fusion.1
  18.3 1.0 slice.57
  19.4 0.2 copy.32
  19.6 0.3 reshape.258
  19.9 3.7 %copy.39 = bf16[64,16,2,4,16]{4,3,2,1,0:T(4,128)(2,1)S(1)} copy(bf16[64,16,2,4,16]{0,2,1,4,3:T(2,128)(2,1)S(1)} %bitcast.33) | data formatting | bytes 524288 | tf_op jit(solution)/shard_map/reshape | solution.py:490
  23.6 1.4 reshape.281.window
  25.0 5.5 %gather_fusion.1 = bf16[20,16,2816]{2,1,0:T(8,128)(2,1)} fusion(bf16[96,16,2816]{2,1,0:T(8,128)(2,1)} %bitcast.36, s32[1024]{0:T(1024)S(1)} %get-tuple-element.37), kind=kCustom, calls=%fused_computation.1 | custom fusion | bytes 3604560 | tf_op jit(solution)/shard_map/jit(_take)/gather | solution.py:454
  30.5 1.8 select_select_fusion
  32.6 60.9 %shard_map.83 = (bf16[2,10,16,3072]{3,2,1,0:T(8,128)(2,1)S(1)}, bf16[8,1024,128]{2,1,0:T(8,128)(2,1)S(1)}) custom-call(bf16[2,10,16,3072]{3,2,1,0:T(8,128)(2,1)S(1)} %pad_maximum_fusion.rows, bf16[1024,128]{1,0:T(8,128)(2,1)S(1)} %reshape.281.window), custom_call_target="tpu_custom_call" | custom-call | tf_op jit(solution)/shard_map/pallas_call | solution.py:222
  93.9 0.2 slice_convert_fusion
  94.1 0.5 multiply_convert_fusion
  94.7 1.1 fusion
  95.8 13.3 %shard_map.84 = bf16[4,64,320]{2,1,0:T(8,128)(2,1)S(1)} custom-call(f32[4,64,320]{2,1,0:T(8,128)S(1)} %pad_maximum_fusion.1.terms), custom_call_target="tpu_custom_call" | custom-call | tf_op jit(solution)/shard_map/pallas_call | solution.py:267
  109.1 0.7 copy.35
  109.9 0.9 copy-done.2
  110.8 22.1 %shard_map.85 = bf16[64,32,128]{2,1,0:T(8,128)(2,1)S(1)} custom-call(s32[20]{0:T(128)S(1)} %select_reduce_fusion.2.slots_ref, bf16[20,16,128]{2,1,0:T(8,128)(2,1)S(1)} %bitcast.30, bf16[128,320]{1,0:T(8,128)(2,1)S(1)} %bitcast.29, bf16[8,1024,128]{2,1,0:T(8,128)(2,1)S(1)} %get-tuple-element.20.blocks), custom_call_target="tpu_custom_call" | custom-call | tf_op jit(solution)/shard_map/pallas_call | solution.py:439
  132.9 0.7 copy.36
  133.8 1.1 copy.37
  134.9 0.7 reshape.263
  135.7 8.7 %reshape_reshape.3.blocks = bf16[4,2,288,1024]{3,2,1,0:T(8,128)(2,1)} reshape(bf16[2304,4,256]{2,1,0:T(4,128)(2,1)} %param.17) | data formatting | bytes 9437184 | tf_op jit(solution)/shard_map/reshape;reshape | solution.py:392
  144.4 2.3 %copy-done.1 = bf16[4,2,288,1024]{3,2,1,0:T(8,128)(2,1)S(1)} copy-done((bf16[4,2,288,1024]{3,2,1,0:T(8,128)(2,1)S(1)}, bf16[4,2,288,1024]{3,2,1,0:T(8,128)(2,1)}, u32[]{:S(2)}) %copy-start.1) | copy-done | bytes 4718616
  146.8 55.6 %shard_map.86 = f32[288,1024]{1,0:T(8,128)S(1)} custom-call(bf16[4,2,288,1024]{3,2,1,0:T(8,128)(2,1)S(1)} %copy-done.1, bf16[256,1024]{1,0:T(8,128)(2,1)S(1)} %copy.38.mine), custom_call_target="tpu_custom_call" | custom-call | tf_op jit(solution)/shard_map/pallas_call | solution.py:375
  202.4 2.0 reshape.264
  (35 shorter events, 2.7 us)
Async XLA Ops:
  0.0 1.1 copy-start
  30.5 1.9 copy-start.3
  109.9 0.9 copy-start.2
  144.4 2.3 %copy-start.1 = (bf16[4,2,288,1024]{3,2,1,0:T(8,128)(2,1)S(1)}, bf16[4,2,288,1024]{3,2,1,0:T(8,128)(2,1)}, u32[]{:S(2)}) copy-start(bf16[4,2,288,1024]{3,2,1,0:T(8,128)(2,1)} %reshape_reshape.3.blocks) | copy-start | bytes 14155780
where the time goes:
time: 205 us; the launch traced here: 204 us
  Pallas kernels  159 us (78%)
  local copies, waits for them, and re-layouts  32.2 us (16%)
  other arithmetic  7.92 us (4%)
  between operations  3.58 us (2%)
    pallas_call x1, Pallas kernels, sum_rows(): pl.pallas_call(functools.partial(rows_kernel, chips, chunks), out_shape=(...  60.9 us
    pallas_call x1, Pallas kernels, couple(): pl.pallas_call(functools.partial(coupling_kernel, chips, shards), out_sha...  55.6 us
    pallas_call x1, Pallas kernels, move(): pl.pallas_call(functools.partial(moved_kernel, own_slots), out_shape=jax....  22.1 us
    pallas_call x1, Pallas kernels, sum_tiles(): pl.pallas_call(functools.partial(tiles_kernel, shards), out_shape=jax.Sha...  13.3 us
    another operation x1, local copies, waits for them, and re-layouts, couple(): blocks.reshape(chips, 2, block[0], depth)  8.7 us
    pallas_call x1, Pallas kernels, gather_table(): pl.pallas_call(functools.partial(table_kernel, groups), out_shape=jax.Sha...  7.45 us
    gather x2, local copies, waits for them, and re-layouts, owned_rows(): jnp.take(blocks, jnp.clip(local_names, 0, local_blocks - 1), axis=0)  6.03 us
    reshape x2, local copies, waits for them, and re-layouts, per_device(): window.transpose(1, 4, 0, 2, 3)  5.11 us

commit v1 on v0

--- a/solution.py
+++ b/solution.py
@@ -76,7 +76,7 @@
     )(table)
 
 
-def rows_kernel(chips, chunks, rows, window, out, blocks,
+def rows_kernel(chips, chunks, pieces, rows, window, whole, out, blocks, flat,
                 own, right_in, left_in, right_out, left_out,
                 own_send, own_recv, right_send, right_recv, left_send, left_recv,
                 done_send, done_recv, far_send, far_recv, near_send, near_recv):
@@ -112,6 +112,14 @@
     blocks[me] = window[...]
 
     def step(i, carry):
+        @pl.when(i < pieces)
+        def _():
+            count, depth = whole.shape[0] // pieces, whole.shape[2]
+            at = pl.ds(pl.multiple_of(i * count, BS), count)
+            part = whole[at].astype(F32)
+            for k in range(whole.shape[1]):
+                flat[at, k * depth:(k + 1) * depth] = part[:, k, :].astype(flat.dtype)
+
         @pl.when(i < chunks)
         def _():
             swap(i).wait_recv()
@@ -214,26 +222,31 @@
         copy.wait_send()
 
 
-def sum_rows(rows, window, groups):
+def sum_rows(rows, window, whole, groups):
     chunks = rows.shape[0] // (2 * BS)
     width = rows.shape[1]
     shape = (2, chunks, BS, width)
     chips = groups // 2
-    summed, blocks = pl.pallas_call(
-        functools.partial(rows_kernel, chips, chunks),
+    units = whole.shape[0] // BS
+    steps = chunks + HOP * (chips - 1)
+    pieces = max(d for d in range(1, steps + 1) if units % d == 0)
+    flat_shape = (whole.shape[0], whole.shape[1] * whole.shape[2])
+    summed, blocks, flat = pl.pallas_call(
+        functools.partial(rows_kernel, chips, chunks, pieces),
         out_shape=(
             jax.ShapeDtypeStruct(shape, rows.dtype),
             jax.ShapeDtypeStruct((groups,) + window.shape, window.dtype),
+            jax.ShapeDtypeStruct(flat_shape, whole.dtype),
         ),
-        in_specs=[VMEM, VMEM],
-        out_specs=(VMEM, VMEM),
+        in_specs=[VMEM, VMEM, VMEM],
+        out_specs=(VMEM, VMEM, VMEM),
         scratch_shapes=[pltpu.VMEM(shape[1:], rows.dtype)] * 5
         + [DMA((chunks,))] * 8
         + [DMA((chips - 1,))] * 2
         + [DMA((chips,))] * 2,
         compiler_params=params(1),
-    )(rows.reshape(shape), window)
-    return summed.reshape(rows.shape), blocks
+    )(rows.reshape(shape), window, whole)
+    return summed.reshape(rows.shape), blocks, flat
 
 
 def tiles_kernel(shards, terms, tiles, held, term_send, term_recv, tile_send, tile_recv):
@@ -283,40 +296,53 @@
     return other
 
 
-def coupling_kernel(chips, shards, blocks, mine, out, kept, moved, near_out, near_in, leaving, arriving,
-                    moved_send, moved_recv, near_send, near_recv, far_send, far_recv):
+def coupling_kernel(chips, shards, blocks, mine, out, kept, moved, total, near_out, near_in,
+                    right_out, right_in, left_out, left_in, moved_send, moved_recv,
+                    near_send, near_recv, right_send, right_recv, left_send, left_recv):
     me, core, chip, partner = place()
     shard = lax.axis_index("aux")
     last = chips - 1
+    after = lax.rem(me + 2, 2 * chips)
+    before = lax.rem(me + 2 * chips - 2, 2 * chips)
     peers = [flipped(shard, k, shards) for k in range(1, shards)]
-    greet([partner] + [lax.rem(chip + k, chips) * 2 + core for k in range(1, chips)], peers)
+    greet([partner, after, before], peers)
 
     def arrival(k):
         return remote(
             mine, moved.at[k], moved_send.at[k], moved_recv.at[k], "aux", flipped(shard, k, shards)
         )
 
-    def target(j):
-        return lax.rem(chip + 1 + j, chips)
-
-    def swap(k, j):
+    def swap(k, to):
         return remote(
-            near_out.at[k, j], near_in.at[k, j], near_send.at[k, j], near_recv.at[k, j], "pair", partner
+            near_out.at[k, to], near_in.at[k, to], near_send.at[k, to], near_recv.at[k, to],
+            "pair", partner,
         )
 
-    def hand_over(k, j):
+    def rightward(k, to):
         return remote(
-            leaving.at[k, j], arriving.at[k, j], far_send.at[k, j], far_recv.at[k, j],
-            "pair", target(j) * 2 + core,
+            right_out.at[k, to], right_in.at[k, to], right_send.at[k, to], right_recv.at[k, to],
+            "pair", after,
+        )
+
+    def leftward(k, to):
+        return remote(
+            left_out.at[k, to], left_in.at[k, to], left_send.at[k, to], left_recv.at[k, to],
+            "pair", before,
         )
 
     for k in range(1, shards):
         arrival(k).start()
     moved[0] = mine[...]
 
-    def product(j, to_core, right):
-        left = blocks[target(j), to_core]
-        return lax.dot_general(left, right, (((1,), (1,)), ((), ())), preferred_element_type=F32)
+    def product(to, to_core, right):
+        return lax.dot_general(
+            blocks[to, to_core], right, (((1,), (1,)), ((), ())), preferred_element_type=F32
+        )
+
+    def chip_sum(k, to):
+        term = product(to, core, moved[k])
+        swap(k, to).wait_recv()
+        return term + near_in[k, to].astype(F32)
 
     def chunk(k, carry):
         @pl.when(k > 0)
@@ -324,40 +350,83 @@
             arrival(k).wait_recv()
 
         def for_partner(j, carry):
-            near_out[k, j] = product(j, 1 - core, moved[k]).astype(near_out.dtype)
-            swap(k, j).start()
+            to = last - j
+            near_out[k, to] = product(to, 1 - core, moved[k]).astype(near_out.dtype)
+            swap(k, to).start()
             return carry
 
         lax.fori_loop(0, chips, for_partner, 0)
 
-        def for_line(j, carry):
-            term = product(j, core, moved[k])
-            swap(k, j).wait_recv()
-            leaving[k, j] = (term + near_in[k, j].astype(F32)).astype(leaving.dtype)
-            hand_over(k, j).start()
+        def for_right(j, carry):
+            to = last - j
+
+            @pl.when(to > chip)
+            def _():
+                total[...] = chip_sum(k, to)
+
+                @pl.when(chip > 0)
+                def _():
+                    rightward(k, to).wait_recv()
+                    total[...] += right_in[k, to].astype(F32)
+
+                right_out[k, to] = total[...].astype(right_out.dtype)
+                rightward(k, to).start()
+
             return carry
 
-        lax.fori_loop(0, last, for_line, 0)
-        term = product(last, core, moved[k])
-        swap(k, last).wait_recv()
-        kept[k] = term + near_in[k, last].astype(F32)
+        lax.fori_loop(0, last, for_right, 0)
+
+        def for_left(to, carry):
+            @pl.when(to < chip)
+            def _():
+                total[...] = chip_sum(k, to)
+
+                @pl.when(chip < last)
+                def _():
+                    leftward(k, to).wait_recv()
+                    total[...] += left_in[k, to].astype(F32)
+
+                left_out[k, to] = total[...].astype(left_out.dtype)
+                leftward(k, to).start()
+
+            return carry
+
+        lax.fori_loop(0, last, for_left, 0)
+        kept[k] = chip_sum(k, chip)
         return carry
 
     lax.fori_loop(0, shards, chunk, 0)
 
     def collect(k, carry):
-        total = kept[k]
-        for j in range(last):
-            hand_over(k, j).wait_recv()
-            total = total + arriving[k, j].astype(F32)
-        width = total.shape[1] // TAUS
+        @pl.when(chip > 0)
+        def _():
+            rightward(k, chip).wait_recv()
+            kept[k] = kept[k] + right_in[k, chip].astype(F32)
+
+        @pl.when(chip < last)
+        def _():
+            leftward(k, chip).wait_recv()
+            kept[k] = kept[k] + left_in[k, chip].astype(F32)
+
+        width = kept.shape[2] // TAUS
         for t in range(TAUS):
             column = (t * shards + flipped(shard, k, shards)) * width
-            out[:, pl.ds(pl.multiple_of(column, width), width)] = total[:, t * width:(t + 1) * width]
-        for j in range(last):
-            hand_over(k, j).wait_send()
-        for j in range(chips):
-            swap(k, j).wait_send()
+            out[:, pl.ds(pl.multiple_of(column, width), width)] = kept[k, :, t * width:(t + 1) * width]
+
+        def sent(to, carry):
+            swap(k, to).wait_send()
+
+            @pl.when(to > chip)
+            def _():
+                rightward(k, to).wait_send()
+
+            @pl.when(to < chip)
+            def _():
+                leftward(k, to).wait_send()
+
+            return carry
+
+        lax.fori_loop(0, chips, sent, 0)
 
         @pl.when(k > 0)
         def _():
@@ -380,14 +449,11 @@
         scratch_shapes=[
             pltpu.VMEM((shards,) + block, F32),
             pltpu.VMEM((shards,) + moved.shape, BF16),
-            pltpu.VMEM((shards, chips) + block, BF16),
-            pltpu.VMEM((shards, chips) + block, BF16),
-            pltpu.VMEM((shards, chips - 1) + block, BF16),
-            pltpu.VMEM((shards, chips - 1) + block, BF16),
+            pltpu.VMEM(block, F32),
         ]
+        + [pltpu.VMEM((shards, chips) + block, BF16)] * 6
         + [DMA((shards,))] * 2
-        + [DMA((shards, chips))] * 2
-        + [DMA((shards, chips - 1))] * 2,
+        + [DMA((shards, chips))] * 6,
         compiler_params=params(3),
     )(blocks.reshape(chips, 2, block[0], depth), moved)
 
@@ -485,10 +551,9 @@
     rows = jnp.concatenate(
         [owned_rows(c_occ, live_names[:, 0], group), owned_rows(c_vir, live_names[:, 1], group)], axis=1
     )
-    flat_blocks = three_center.reshape(three_center.shape[0], own_slots * BS * BS)
     window = three_center[:WIN_DEV].reshape(PAIRS, WIN_DEV // PAIRS, own_slots, BS, BS)
     window = window.transpose(1, 4, 0, 2, 3).reshape(WIN_DEV // PAIRS * BS, PAIRS * own_slots * BS)
-    rows, blocks = sum_rows(rows, window, groups)
+    rows, blocks, flat_blocks = sum_rows(rows, window, three_center, groups)
     before = jnp.sum(jnp.where(jnp.arange(groups) < group, counts, 0))
     picks = [jnp.minimum(before + k, live_total - 1) for k in range(own_slots)]
     n_occ = c_occ.shape[1]

time: 205 us -> 212 us (1.034)
  Pallas kernels: 159 us -> 173 us
  local copies, waits for them, and re-layouts: 32.2 us -> 25 us
    pallas_call x1, Pallas kernels: 55.6 us -> 67.3 us  [couple(): pl.pallas_call(functools.partial(coupling_kernel, chips, shards), out_sha...]
    another operation x1 -> x0, local copies, waits for them, and re-layouts: 8.7 us -> none  [couple(): blocks.reshape(chips, 2, block[0], depth)]
    pallas_call x1, Pallas kernels: 60.9 us -> 63.3 us  [sum_rows(): pl.pallas_call(functools.partial(rows_kernel, chips, chunks, pieces), out...]
    unnamed x9 -> x11, local copies, waits for them, and re-layouts: 4.42 us -> 5.95 us
where the time goes in v1:
time: 212 us; the launch traced here: 211 us
  Pallas kernels  173 us (82%)
  local copies, waits for them, and re-layouts  25 us (12%)
  other arithmetic  7.92 us (4%)
  between operations  3.6 us (2%)
    pallas_call x1, Pallas kernels, couple(): pl.pallas_call(functools.partial(coupling_kernel, chips, shards), out_sha...  67.3 us
    pallas_call x1, Pallas kernels, sum_rows(): pl.pallas_call(functools.partial(rows_kernel, chips, chunks, pieces), out...  63.3 us
    pallas_call x1, Pallas kernels, move(): pl.pallas_call(functools.partial(moved_kernel, own_slots), out_shape=jax....  22.1 us
    pallas_call x1, Pallas kernels, sum_tiles(): pl.pallas_call(functools.partial(tiles_kernel, shards), out_shape=jax.Sha...  13.3 us
    pallas_call x1, Pallas kernels, gather_table(): pl.pallas_call(functools.partial(table_kernel, groups), out_shape=jax.Sha...  7.45 us
    gather x2, local copies, waits for them, and re-layouts, owned_rows(): jnp.take(blocks, jnp.clip(local_names, 0, local_blocks - 1), axis=0)  6.03 us
    unnamed x11, local copies, waits for them, and re-layouts  5.95 us
    reshape x2, local copies, waits for them, and re-layouts, per_device(): window.transpose(1, 4, 0, 2, 3)  5.11 us

profile of v1, /device:TPU:0, one launch (start us, length us, event | category | flops | bytes accessed | tf_op | source)
XLA Modules:
  0.0 211.3 jit_solution(16292566971466762145)
XLA Ops:
  0.7 0.4 copy-done
  1.2 0.7 broadcast_multiply_fusion
  1.8 0.8 multiply_exponential_fusion.1
  2.6 0.8 copy.30
  3.5 0.8 multiply_exponential_fusion
  4.3 7.4 %shard_map.82 = s32[8,8,128]{2,1,0:T(8,128)S(1)} custom-call(s32[8,128]{1,0:T(8,128)S(1)} %scatter.4.mine), custom_call_target="tpu_custom_call" | custom-call | tf_op jit(solution)/shard_map/pallas_call | solution.py:69
  12.0 0.6 fusion.20
  15.8 0.4 select_reduce_fusion
  17.0 0.6 gather_fusion
  17.5 0.8 select_select_fusion.1
  18.3 1.0 slice.57
  19.4 0.2 copy.32
  19.6 0.3 reshape.262
  19.9 3.7 %copy.39 = bf16[64,16,2,4,16]{4,3,2,1,0:T(4,128)(2,1)S(1)} copy(bf16[64,16,2,4,16]{0,2,1,4,3:T(2,128)(2,1)S(1)} %bitcast.35) | data formatting | bytes 524288 | tf_op jit(solution)/shard_map/reshape | solution.py:555
  23.6 1.4 reshape.286.window
  25.0 5.5 %gather_fusion.1 = bf16[20,16,2816]{2,1,0:T(8,128)(2,1)} fusion(bf16[96,16,2816]{2,1,0:T(8,128)(2,1)} %bitcast.38, s32[1024]{0:T(1024)S(1)} %get-tuple-element.39), kind=kCustom, calls=%fused_computation.1 | custom fusion | bytes 3604560 | tf_op jit(solution)/shard_map/jit(_take)/gather | solution.py:520
  30.5 1.8 select_select_fusion
  32.6 63.3 %shard_map.83 = (bf16[2,10,16,3072]{3,2,1,0:T(8,128)(2,1)S(1)}, bf16[8,1024,128]{2,1,0:T(8,128)(2,1)S(1)}, bf16[2304,1024]{1,0:T(8,128)(2,1)S(1)}) custom-call(bf16[2,10,16,3072]{3,2,1,0:T(8,128)(2,1)S(1)} %pad_maximum_fusion.rows, bf16[1024,128]{1,0:T(8,128)(2,1)S(1)} %reshape.286.window, bf16[2304,4,256]{2,1,0:T(4,128)(2,1)} %whole.1), custom_call_target="tpu_custom_call" | custom-call | tf_op jit(solution)/shard_map/pallas_call | solution.py:234
  96.2 0.2 slice_convert_fusion
  96.4 1.5 copy-done.1
  98.0 0.5 multiply_convert_fusion
  98.5 1.1 fusion
  99.7 13.3 %shard_map.84 = bf16[4,64,320]{2,1,0:T(8,128)(2,1)S(1)} custom-call(f32[4,64,320]{2,1,0:T(8,128)S(1)} %pad_maximum_fusion.1.terms), custom_call_target="tpu_custom_call" | custom-call | tf_op jit(solution)/shard_map/pallas_call | solution.py:280
  113.0 0.7 copy.35
  113.8 0.9 copy-done.3
  114.6 22.1 %shard_map.85 = bf16[64,32,128]{2,1,0:T(8,128)(2,1)S(1)} custom-call(s32[20]{0:T(128)S(1)} %select_reduce_fusion.2.slots_ref, bf16[20,16,128]{2,1,0:T(8,128)(2,1)S(1)} %bitcast.32, bf16[128,320]{1,0:T(8,128)(2,1)S(1)} %bitcast.31, bf16[8,1024,128]{2,1,0:T(8,128)(2,1)S(1)} %get-tuple-element.22.blocks), custom_call_target="tpu_custom_call" | custom-call | tf_op jit(solution)/shard_map/pallas_call | solution.py:505
  136.8 0.7 copy.36
  137.6 1.1 copy.37
  138.7 0.7 reshape.268
  139.6 2.3 %copy-done.2 = bf16[2304,1024]{1,0:T(8,128)(2,1)S(1)} copy-done((bf16[2304,1024]{1,0:T(8,128)(2,1)S(1)}, bf16[2304,1024]{1,0:T(8,128)(2,1)}, u32[]{:S(2)}) %copy-start.2) | copy-done | bytes 4718616
  141.9 67.3 %shard_map.86 = f32[288,1024]{1,0:T(8,128)S(1)} custom-call(bf16[4,2,288,1024]{3,2,1,0:T(8,128)(2,1)S(1)} %bitcast.28, bf16[256,1024]{1,0:T(8,128)(2,1)S(1)} %copy.38.mine), custom_call_target="tpu_custom_call" | custom-call | tf_op jit(solution)/shard_map/pallas_call | solution.py:444
  209.3 2.0 reshape.269
  (36 shorter events, 2.7 us)
Async XLA Ops:
  0.0 1.1 copy-start
  30.5 1.9 copy-start.4
  95.8 2.1 %copy-start.1 = (bf16[2304,1024]{1,0:T(8,128)(2,1)}, bf16[2304,1024]{1,0:T(8,128)(2,1)S(1)}, u32[]{:S(2)}) copy-start(bf16[2304,1024]{1,0:T(8,128)(2,1)S(1)} %get-tuple-element.20) | copy-start | bytes 14155780
  113.8 0.9 copy-start.3
  139.6 2.3 %copy-start.2 = (bf16[2304,1024]{1,0:T(8,128)(2,1)S(1)}, bf16[2304,1024]{1,0:T(8,128)(2,1)}, u32[]{:S(2)}) copy-start(bf16[2304,1024]{1,0:T(8,128)(2,1)} %copy-done.1) | copy-start | bytes 14155780
